TPU v7x, 32 devices: a whole 2x2x4 slice. The times are simulated.
32 devices in a mesh: blk: 16 (over z, x, core), tgt: 2 (over y).
Axes of the slice: x: 2, y: 2, z: 4, core: 2. Of those that a mesh axis runs over, the one named last changes fastest.
Arguments:
- queries: bfloat16 [4096, 1024], P(('blk', 'tgt')), may hold values from -6 to 6
- keys: bfloat16 [1024, 1024], P('blk'), may hold values from -6 to 6
- values: bfloat16 [1024, 1024], P('blk'), may hold values from -6 to 6
- out_weight: bfloat16 [1024, 1024], P('tgt'), may hold values from -0.1875 to 0.1875
- out_grad: bfloat16 [4096, 1024], P(('blk', 'tgt')), may hold values from -6 to 6
Outputs:
- outputs: bfloat16 [4096, 1024], P(('blk', 'tgt'))
- query_grad: bfloat16 [4096, 1024], P(('blk', 'tgt'))
- key_grad: bfloat16 [1024, 1024], P('blk', 'tgt')
- value_grad: bfloat16 [1024, 1024], P('blk', 'tgt')
- weight_grad: bfloat16 [1024, 1024], P('tgt', 'blk')
All inputs are finite; a program needn't handle non-finite values.
Results may differ from a plain program's by a relative error of at most 0.017.
Values may be sent and summed in bfloat16 or wider, within the bound.
A program may use at most 64 MiB of HBM per device.

v0:
```python
import jax
import jax.numpy as jnp
from jax import lax
from jax.sharding import PartitionSpec as P

D = 1024
HEADS = 16
HD = 64
WIN = 5
SRC_DEV = 64


def shifted(value, axis, steps):
    count = lax.axis_size(axis)
    pairs = [(source, (source + steps) % count) for source in range(count)]
    return lax.ppermute(value, axis, pairs)


def for_sending(value):
    return jax.tree.map(lambda a: a.astype(jnp.bfloat16) if a.dtype == jnp.float32 else a, value)


def head_block(query_cols, key_cols, value_cols, grad_cols, group_heads):
    scale = HD ** (-0.5)
    count = query_cols.shape[0]
    width = key_cols.shape[0]
    query_heads = query_cols.reshape(count, group_heads, HD)
    key_heads = key_cols.reshape(width, group_heads, HD)
    value_heads = value_cols.reshape(width, group_heads, HD)
    grad_heads = grad_cols.reshape(count, group_heads, HD)
    scores = (
        jnp.einsum("rhd,jhd->hrj", query_heads, key_heads, preferred_element_type=jnp.float32)
        * scale
    )
    top = jnp.max(scores, axis=-1, keepdims=True)
    expo = jnp.exp(scores - top)
    probs = expo / jnp.sum(expo, axis=-1, keepdims=True)
    probs_low = probs.astype(jnp.bfloat16)
    attended = jnp.einsum(
        "hrj,jhd->rhd", probs_low, value_heads, preferred_element_type=jnp.float32
    )
    attended = attended.reshape(count, group_heads * HD).astype(jnp.bfloat16)
    prob_grad = jnp.einsum(
        "rhd,jhd->hrj", grad_heads, value_heads, preferred_element_type=jnp.float32
    )
    center = jnp.sum(probs * prob_grad, axis=-1, keepdims=True)
    score_grad = (scale * probs * (prob_grad - center)).astype(jnp.bfloat16)
    query_grad = jnp.einsum(
        "hrj,jhd->rhd", score_grad, key_heads, preferred_element_type=jnp.float32
    )
    query_grad = query_grad.reshape(count, group_heads * HD).astype(jnp.bfloat16)
    key_part = jnp.einsum(
        "hrj,rhd->jhd", score_grad, query_heads, preferred_element_type=jnp.float32
    )
    value_part = jnp.einsum(
        "hrj,rhd->jhd", probs_low, grad_heads, preferred_element_type=jnp.float32
    )
    return (
        attended,
        query_grad,
        key_part.reshape(width, group_heads * HD),
        value_part.reshape(width, group_heads * HD),
    )


def local(queries, keys, values, out_weight, out_grad):
    full_weight = lax.all_gather(out_weight, "tgt", axis=0, tiled=True)
    current = (keys, values)
    key_list = [keys]
    value_list = [values]
    for step in range(1, WIN):
        current = shifted((current[0], current[1]), "blk", 1)
        key_list.append(current[0])
        value_list.append(current[1])
    seen_keys = jnp.concatenate(key_list, axis=0)
    seen_values = jnp.concatenate(value_list, axis=0)
    attended_grad = jnp.dot(out_grad, full_weight.T, preferred_element_type=jnp.float32).astype(
        jnp.bfloat16
    )
    group_heads = min(4, HEADS)
    span = group_heads * HD
    pieces = []
    for first in range(0, D, span):
        pieces.append(
            head_block(
                queries[:, first : first + span],
                seen_keys[:, first : first + span],
                seen_values[:, first : first + span],
                attended_grad[:, first : first + span],
                group_heads,
            )
        )
    attended = jnp.concatenate([p[0] for p in pieces], axis=1)
    query_grad = jnp.concatenate([p[1] for p in pieces], axis=1)
    key_part = jnp.concatenate([p[2] for p in pieces], axis=1)
    value_part = jnp.concatenate([p[3] for p in pieces], axis=1)
    outputs = jnp.dot(attended, full_weight, preferred_element_type=jnp.float32).astype(
        jnp.bfloat16
    )
    rows = SRC_DEV
    carried = (key_part[(WIN - 1) * rows : WIN * rows], value_part[(WIN - 1) * rows : WIN * rows])
    for step in range(WIN - 2, -1, -1):
        moved = shifted((for_sending(carried[0]), for_sending(carried[1])), "blk", -1)
        carried = (
            moved[0] + key_part[step * rows : (step + 1) * rows],
            moved[1] + value_part[step * rows : (step + 1) * rows],
        )
    key_total, value_total = carried
    key_grad, value_grad = (
        lax.psum_scatter(
            key_total.astype(jnp.bfloat16), "tgt", scatter_dimension=1, tiled=True
        ).astype(jnp.float32),
        lax.psum_scatter(
            value_total.astype(jnp.bfloat16), "tgt", scatter_dimension=1, tiled=True
        ).astype(jnp.float32),
    )
    tile_sum = lax.psum_scatter(
        jnp.einsum("rc,re->ce", attended, out_grad, preferred_element_type=jnp.float32).astype(
            jnp.bfloat16
        ),
        "tgt",
        scatter_dimension=0,
        tiled=True,
    ).astype(jnp.float32)
    weight_grad = lax.psum_scatter(tile_sum, "blk", scatter_dimension=1, tiled=True)
    return (
        outputs,
        query_grad,
        key_grad.astype(jnp.bfloat16),
        value_grad.astype(jnp.bfloat16),
        weight_grad.astype(jnp.bfloat16),
    )


def solution(mesh):
    return jax.shard_map(
        local,
        mesh=mesh,
        in_specs=(
            P(("blk", "tgt"), None),
            P("blk", None),
            P("blk", None),
            P("tgt", None),
            P(("blk", "tgt"), None),
        ),
        out_specs=(
            P(("blk", "tgt"), None),
            P(("blk", "tgt"), None),
            P("blk", "tgt"),
            P("blk", "tgt"),
            P("tgt", "blk"),
        ),
        check_vma=False,
    )
```

profile of v0, /device:TPU:0, one launch (start us, length us, event | category | flops | bytes accessed | tf_op | source)
XLA Modules:
  0.0 179.5 jit_solution(15206731886575066169)
XLA Ops:
  7.2 0.7 all-gather.2.cloned.1.call-update
  8.5 2.6 %collective-permute-start = (bf16[64,1024]{1,0:T(8,128)(2,1)}, bf16[64,1024]{1,0:T(8,128)(2,1)S(1)}, u32[]{:S(2)}, u32[]{:S(2)}) collective-permute-start(bf16[64,1024]{1,0:T(8,128)(2,1)} %param.7), channel_id=1, source_target_pairs={{0,2},{2,4},{4,6},{6,8},{8,10},{10,12},{12,14},{14,16},{16,18},{18... | collective-permute-start | bytes 393224 | tf_op jit(solution)/shard_map/ppermute | solution.py:16
  11.1 1.0 fusion.49
  12.6 3.7 %collective-permute-done.4 = bf16[64,1024]{1,0:T(8,128)(2,1)S(1)} collective-permute-done((bf16[64,1024]{1,0:T(8,128)(2,1)}, bf16[64,1024]{1,0:T(8,128)(2,1)S(1)}, u32[]{:S(2)}, u32[]{:S(2)}) %collective-permute-start.4) | collective-permute-done | bytes 131104 | tf_op jit(solution)/shard_map/ppermute | solution.py:16
  16.3 1.4 collective-permute-done
  17.8 5.7 %collective-permute-done.5 = bf16[64,1024]{1,0:T(8,128)(2,1)S(1)} collective-permute-done((bf16[64,1024]{1,0:T(8,128)(2,1)S(1)}, bf16[64,1024]{1,0:T(8,128)(2,1)S(1)}, u32[]{:S(2)}, u32[]{:S(2)}) %collective-permute-start.5) | collective-permute-done | bytes 131104 | tf_op jit(solution)/shard_map/ppermute | solution.py:16
  23.4 1.4 collective-permute-done.1
  24.8 5.7 %collective-permute-done.6 = bf16[64,1024]{1,0:T(8,128)(2,1)S(1)} collective-permute-done((bf16[64,1024]{1,0:T(8,128)(2,1)S(1)}, bf16[64,1024]{1,0:T(8,128)(2,1)S(1)}, u32[]{:S(2)}, u32[]{:S(2)}) %collective-permute-start.6) | collective-permute-done | bytes 131104 | tf_op jit(solution)/shard_map/ppermute | solution.py:16
  30.5 1.4 collective-permute-done.2
  31.9 5.7 %collective-permute-done.7 = bf16[64,1024]{1,0:T(8,128)(2,1)S(1)} collective-permute-done((bf16[64,1024]{1,0:T(8,128)(2,1)S(1)}, bf16[64,1024]{1,0:T(8,128)(2,1)S(1)}, u32[]{:S(2)}, u32[]{:S(2)}) %collective-permute-start.7) | collective-permute-done | bytes 131104 | tf_op jit(solution)/shard_map/ppermute | solution.py:16
  40.8 1.2 fusion.51
  42.6 1.3 fusion.50
  44.5 1.3 fusion.53
  46.4 2.0 %convolution_convert_fusion = bf16[1024,1024]{1,0:T(8,128)(2,1)} fusion(bf16[128,1024]{1,0:T(8,128)(2,1)S(1)} %copy-done, bf16[128,256]{0,1:T(8,128)(2,1)S(1)} %bitcast.219, bf16[128,256]{0,1:T(8,128)(2,1)S(1)} %bitcast.217, bf16[128,256]{0,1:T(8,128)(2,1)S(1)} %bitcast.215, bf16[128,256]{0,1:T(8,128)(2,1)S(1)} %bitcast.221), kind=kOutput, calls=%fused_computation.4 | convolution fusion | flops 270532608 | bytes 2621440 | tf_op jit(solution)/shard_map/rc,re->ce/dot_general | solution.py:118
  48.5 2.4 %convolution_convert_fusion.1 = bf16[128,1024]{1,0:T(8,128)(2,1)S(1)} fusion(bf16[128,1024]{1,0:T(8,128)(2,1)S(1)} %copy-done, bf16[1024,1024]{1,0:T(8,128)(2,1)} %all-gather.2.cloned.1.call-done), kind=kOutput, calls=%fused_computation.23 | convolution fusion | flops 268566528 | bytes 2621440 | tf_op jit(solution)/shard_map/dot_general | solution.py:77
  53.4 0.7 copy.89
  55.3 1.3 multiply_reduce_fusion.1
  57.7 0.7 copy.90
  59.1 0.9 copy.99
  60.3 0.8 copy-done.10
  62.2 0.7 copy.91
  62.9 16.6 %reduce-scatter.11.cloned.1.call-done = bf16[512,1024]{1,0:T(8,128)(2,1)} async-done(((bf16[1024,1024]{1,0:T(8,128)(2,1)}), bf16[512,1024]{1,0:T(8,128)(2,1)}) %reduce-scatter.11.cloned.1.call-update) | async-done | bytes 1048592 | tf_op jit(solution)/shard_map/reduce_scatter | solution.py:117
  79.5 2.6 %copy.101 = f32[512,1024]{0,1:T(8,128)} copy(bf16[512,1024]{1,0:T(8,128)(2,1)} %reduce-scatter.11.cloned.1.call-done) | data formatting | bytes 3145728
  83.5 0.9 copy.96
  84.4 1.3 pad_maximum_fusion.1
  85.7 0.7 slice.154
  86.5 3.7 %collective-permute-start.12 = (bf16[64,1024]{1,0:T(8,128)(2,1)}, bf16[64,1024]{1,0:T(8,128)(2,1)}, u32[]{:S(2)}, u32[]{:S(2)}) collective-permute-start(bf16[64,1024]{1,0:T(8,128)(2,1)} %slice.154), channel_id=1, source_target_pairs={{0,30},{2,0},{4,2},{6,4},{8,6},{10,8},{12,10},{14,12},{16,14},{18,... | collective-permute-start | bytes 393224 | tf_op jit(solution)/shard_map/ppermute | solution.py:16
  90.6 0.7 copy-done.21
  91.5 0.9 copy.92
  92.8 1.1 pad_maximum_fusion
  93.9 0.7 collective-permute-start.8
  94.6 0.9 fusion.19
  95.6 3.0 %collective-permute-start.13 = (bf16[64,1024]{1,0:T(8,128)(2,1)S(1)}, bf16[64,1024]{1,0:T(8,128)(2,1)S(1)}, u32[]{:S(2)}, u32[]{:S(2)}) collective-permute-start(bf16[64,1024]{1,0:T(8,128)(2,1)S(1)} %fusion.19), channel_id=1, source_target_pairs={{0,30},{2,0},{4,2},{6,4},{8,6},{10,8},{12,10},{14,12},{16,14},{18,... | collective-permute-start | bytes 393224 | tf_op jit(solution)/shard_map/ppermute | solution.py:16
  98.6 3.2 %collective-permute-start.9 = (bf16[64,1024]{1,0:T(8,128)(2,1)S(1)}, bf16[64,1024]{1,0:T(8,128)(2,1)S(1)}, u32[]{:S(2)}, u32[]{:S(2)}) collective-permute-start(bf16[64,1024]{1,0:T(8,128)(2,1)S(1)} %fusion.23), channel_id=1, source_target_pairs={{0,30},{2,0},{4,2},{6,4},{8,6},{10,8},{12,10},{14,12},{16,14},{18,... | collective-permute-start | bytes 393224 | tf_op jit(solution)/shard_map/ppermute | solution.py:16
  101.9 3.8 %collective-permute-start.14 = (bf16[64,1024]{1,0:T(8,128)(2,1)S(1)}, bf16[64,1024]{1,0:T(8,128)(2,1)S(1)}, u32[]{:S(2)}, u32[]{:S(2)}) collective-permute-start(bf16[64,1024]{1,0:T(8,128)(2,1)S(1)} %fusion.18), channel_id=1, source_target_pairs={{0,30},{2,0},{4,2},{6,4},{8,6},{10,8},{12,10},{14,12},{16,14},{18,... | collective-permute-start | bytes 393224 | tf_op jit(solution)/shard_map/ppermute | solution.py:16
  105.7 3.3 %collective-permute-start.10 = (bf16[64,1024]{1,0:T(8,128)(2,1)S(1)}, bf16[64,1024]{1,0:T(8,128)(2,1)S(1)}, u32[]{:S(2)}, u32[]{:S(2)}) collective-permute-start(bf16[64,1024]{1,0:T(8,128)(2,1)S(1)} %fusion.22), channel_id=1, source_target_pairs={{0,30},{2,0},{4,2},{6,4},{8,6},{10,8},{12,10},{14,12},{16,14},{18,... | collective-permute-start | bytes 393224 | tf_op jit(solution)/shard_map/ppermute | solution.py:16
  109.1 3.8 %collective-permute-start.15 = (bf16[64,1024]{1,0:T(8,128)(2,1)S(1)}, bf16[64,1024]{1,0:T(8,128)(2,1)S(1)}, u32[]{:S(2)}, u32[]{:S(2)}) collective-permute-start(bf16[64,1024]{1,0:T(8,128)(2,1)S(1)} %fusion.17), channel_id=1, source_target_pairs={{0,30},{2,0},{4,2},{6,4},{8,6},{10,8},{12,10},{14,12},{16,14},{18,... | collective-permute-start | bytes 393224 | tf_op jit(solution)/shard_map/ppermute | solution.py:16
  113.0 3.7 %collective-permute-start.11 = (bf16[64,1024]{1,0:T(8,128)(2,1)S(1)}, bf16[64,1024]{1,0:T(8,128)(2,1)S(1)}, u32[]{:S(2)}, u32[]{:S(2)}) collective-permute-start(bf16[64,1024]{1,0:T(8,128)(2,1)S(1)} %fusion.21), channel_id=1, source_target_pairs={{0,30},{2,0},{4,2},{6,4},{8,6},{10,8},{12,10},{14,12},{16,14},{18,... | collective-permute-start | bytes 393224 | tf_op jit(solution)/shard_map/ppermute | solution.py:16
  116.7 1.6 fusion.16
  118.4 0.7 pad_maximum_fusion.3
  119.2 1.1 collective-permute-done.11
  120.2 1.6 fusion.20
  121.9 1.2 convolution_convert_fusion.2
  123.1 25.0 %reduce-scatter.13.cloned.1.call-done = f32[64,512]{1,0:T(8,128)} async-done(((f32[1024,512]{1,0:T(8,128)}), f32[64,512]{1,0:T(8,128)}) %reduce-scatter.13.cloned.1.call-update) | async-done | bytes 131088
  148.1 1.0 copy.102
  149.2 0.7 copy.100
  149.9 10.2 %reduce-scatter.9.cloned.1.call-done = bf16[64,512]{1,0:T(8,128)(2,1)} async-done(((bf16[64,1024]{1,0:T(8,128)(2,1)}), bf16[64,512]{1,0:T(8,128)(2,1)}) %reduce-scatter.9.cloned.1.call-update) | async-done | bytes 65552 | tf_op jit(solution)/shard_map/reduce_scatter | solution.py:113
  160.1 12.9 %reduce-scatter.7.cloned.1.call-done = bf16[64,512]{1,0:T(8,128)(2,1)} async-done(((bf16[64,1024]{1,0:T(8,128)(2,1)}), bf16[64,512]{1,0:T(8,128)(2,1)}) %reduce-scatter.7.cloned.1.call-update) | async-done | bytes 65552 | tf_op jit(solution)/shard_map/reduce_scatter | solution.py:110
  (164 shorter events, 15.4 us)
Async XLA Ops:
  7.2 39.2 %copy-start = (bf16[128,1024]{1,0:T(8,128)(2,1)S(1)}, bf16[128,1024]{1,0:T(8,128)(2,1)}, u32[]{:S(2)}) copy-start(bf16[128,1024]{1,0:T(8,128)(2,1)} %param.9) | copy-start | bytes 786436
  7.2 4.9 %copy-start.34 = (bf16[64,1024]{1,0:T(8,128)(2,1)S(1)}, bf16[64,1024]{1,0:T(8,128)(2,1)}, u32[]{:S(2)}) copy-start(bf16[64,1024]{1,0:T(8,128)(2,1)} %param.6) | copy-start | bytes 393220
  7.2 5.4 %copy-start.35 = (bf16[64,1024]{1,0:T(8,128)(2,1)S(1)}, bf16[64,1024]{1,0:T(8,128)(2,1)}, u32[]{:S(2)}) copy-start(bf16[64,1024]{1,0:T(8,128)(2,1)} %param.7) | copy-start | bytes 393220
  7.2 41.3 %all-gather.2.cloned.1.call-start = ((), (), s32[]{:S(2)}) async-start(), calls=%async_computation.4 | async-start | bytes 3145728 | tf_op jit(solution)/shard_map/all_gather | solution.py:67
  7.9 71.6 %reduce-scatter.11.cloned.1.call-start = ((), (), s32[]{:S(2)}) async-start(), calls=%async_computation.7 | async-start | bytes 3145728 | tf_op jit(solution)/shard_map/reduce_scatter | solution.py:117
  8.0 8.3 %collective-permute-start.4 = (bf16[64,1024]{1,0:T(8,128)(2,1)}, bf16[64,1024]{1,0:T(8,128)(2,1)S(1)}, u32[]{:S(2)}, u32[]{:S(2)}) collective-permute-start(bf16[64,1024]{1,0:T(8,128)(2,1)} %param.6), channel_id=1, source_target_pairs={{0,2},{2,4},{4,6},{6,8},{8,10},{10,12},{12,14},{14,16},{16,18},{18... | collective-permute-start | bytes 393224 | tf_op jit(solution)/shard_map/ppermute | solution.py:16
  8.5 9.2 %collective-permute-start = (bf16[64,1024]{1,0:T(8,128)(2,1)}, bf16[64,1024]{1,0:T(8,128)(2,1)S(1)}, u32[]{:S(2)}, u32[]{:S(2)}) collective-permute-start(bf16[64,1024]{1,0:T(8,128)(2,1)} %param.7), channel_id=1, source_target_pairs={{0,2},{2,4},{4,6},{6,8},{8,10},{10,12},{12,14},{14,16},{16,18},{18... | collective-permute-start | bytes 393224 | tf_op jit(solution)/shard_map/ppermute | solution.py:16
  12.2 33.6 %copy-start.19 = (bf16[128,256]{0,1:T(8,128)(2,1)}, bf16[128,256]{0,1:T(8,128)(2,1)S(1)}, u32[]{:S(2)}) copy-start(bf16[128,256]{0,1:T(8,128)(2,1)S(1)} %copy.74) | copy-start | bytes 196612
  12.4 31.5 %copy-start.22 = (bf16[128,256]{0,1:T(8,128)(2,1)}, bf16[128,256]{0,1:T(8,128)(2,1)S(1)}, u32[]{:S(2)}) copy-start(bf16[128,256]{0,1:T(8,128)(2,1)S(1)} %copy.83) | copy-start | bytes 196612
  12.6 29.5 %copy-start.24 = (bf16[128,256]{0,1:T(8,128)(2,1)}, bf16[128,256]{0,1:T(8,128)(2,1)S(1)}, u32[]{:S(2)}) copy-start(bf16[128,256]{0,1:T(8,128)(2,1)S(1)} %copy.80) | copy-start | bytes 196612
  16.3 7.1 %collective-permute-start.5 = (bf16[64,1024]{1,0:T(8,128)(2,1)S(1)}, bf16[64,1024]{1,0:T(8,128)(2,1)S(1)}, u32[]{:S(2)}, u32[]{:S(2)}) collective-permute-start(bf16[64,1024]{1,0:T(8,128)(2,1)S(1)} %collective-permute-done.4), channel_id=1, source_target_pairs={{0,2},{2,4},{4,6},{6,8},{8,10},{10,12},{12,14},{14,16},{16,18},{18... | collective-permute-start | bytes 393224 | tf_op jit(solution)/shard_map/ppermute | solution.py:16
  17.7 7.1 %collective-permute-start.1 = (bf16[64,1024]{1,0:T(8,128)(2,1)S(1)}, bf16[64,1024]{1,0:T(8,128)(2,1)S(1)}, u32[]{:S(2)}, u32[]{:S(2)}) collective-permute-start(bf16[64,1024]{1,0:T(8,128)(2,1)S(1)} %collective-permute-done), channel_id=1, source_target_pairs={{0,2},{2,4},{4,6},{6,8},{8,10},{10,12},{12,14},{14,16},{16,18},{18... | collective-permute-start | bytes 393224 | tf_op jit(solution)/shard_map/ppermute | solution.py:16
  23.4 7.1 %collective-permute-start.6 = (bf16[64,1024]{1,0:T(8,128)(2,1)S(1)}, bf16[64,1024]{1,0:T(8,128)(2,1)S(1)}, u32[]{:S(2)}, u32[]{:S(2)}) collective-permute-start(bf16[64,1024]{1,0:T(8,128)(2,1)S(1)} %collective-permute-done.5), channel_id=1, source_target_pairs={{0,2},{2,4},{4,6},{6,8},{8,10},{10,12},{12,14},{14,16},{16,18},{18... | collective-permute-start | bytes 393224 | tf_op jit(solution)/shard_map/ppermute | solution.py:16
  24.8 7.1 %collective-permute-start.2 = (bf16[64,1024]{1,0:T(8,128)(2,1)S(1)}, bf16[64,1024]{1,0:T(8,128)(2,1)S(1)}, u32[]{:S(2)}, u32[]{:S(2)}) collective-permute-start(bf16[64,1024]{1,0:T(8,128)(2,1)S(1)} %collective-permute-done.1), channel_id=1, source_target_pairs={{0,2},{2,4},{4,6},{6,8},{8,10},{10,12},{12,14},{14,16},{16,18},{18... | collective-permute-start | bytes 393224 | tf_op jit(solution)/shard_map/ppermute | solution.py:16
  30.5 7.1 %collective-permute-start.7 = (bf16[64,1024]{1,0:T(8,128)(2,1)S(1)}, bf16[64,1024]{1,0:T(8,128)(2,1)S(1)}, u32[]{:S(2)}, u32[]{:S(2)}) collective-permute-start(bf16[64,1024]{1,0:T(8,128)(2,1)S(1)} %collective-permute-done.6), channel_id=1, source_target_pairs={{0,2},{2,4},{4,6},{6,8},{8,10},{10,12},{12,14},{14,16},{16,18},{18... | collective-permute-start | bytes 393224 | tf_op jit(solution)/shard_map/ppermute | solution.py:16
  31.9 7.1 %collective-permute-start.3 = (bf16[64,1024]{1,0:T(8,128)(2,1)S(1)}, bf16[64,1024]{1,0:T(8,128)(2,1)S(1)}, u32[]{:S(2)}, u32[]{:S(2)}) collective-permute-start(bf16[64,1024]{1,0:T(8,128)(2,1)S(1)} %collective-permute-done.2), channel_id=1, source_target_pairs={{0,2},{2,4},{4,6},{6,8},{8,10},{10,12},{12,14},{14,16},{16,18},{18... | collective-permute-start | bytes 393224 | tf_op jit(solution)/shard_map/ppermute | solution.py:16
  38.0 20.5 %copy-start.4 = (bf16[320,256]{0,1:T(8,128)(2,1)}, bf16[320,256]{0,1:T(8,128)(2,1)S(1)}, u32[]{:S(2)}) copy-start(bf16[320,256]{0,1:T(8,128)(2,1)S(1)} %copy.82) | copy-start | bytes 491524
  38.2 16.0 %copy-start.6 = (bf16[320,256]{0,1:T(8,128)(2,1)}, bf16[320,256]{0,1:T(8,128)(2,1)S(1)}, u32[]{:S(2)}) copy-start(bf16[320,256]{0,1:T(8,128)(2,1)S(1)} %copy.79) | copy-start | bytes 491524
  39.2 6.6 %copy-start.29 = (bf16[320,256]{0,1:T(8,128)(2,1)}, bf16[320,256]{0,1:T(8,128)(2,1)S(1)}, u32[]{:S(2)}) copy-start(bf16[320,256]{0,1:T(8,128)(2,1)S(1)} %copy.72) | copy-start | bytes 491524
  39.6 2.5 %copy-start.31 = (bf16[320,256]{0,1:T(8,128)(2,1)}, bf16[320,256]{0,1:T(8,128)(2,1)S(1)}, u32[]{:S(2)}) copy-start(bf16[320,256]{0,1:T(8,128)(2,1)S(1)} %copy.78) | copy-start | bytes 491524
  42.6 3.7 %copy-start.13 = (bf16[4,64,128]{2,1,0:T(8,128)(2,1)}, bf16[4,64,128]{2,1,0:T(8,128)(2,1)S(1)}, u32[]{:S(2)}) copy-start(bf16[4,64,128]{2,1,0:T(8,128)(2,1)S(1)} %convolution_convert_fusion.8) | copy-start | bytes 196612
  44.5 1.9 %copy-start.15 = (bf16[4,64,128]{2,1,0:T(8,128)(2,1)}, bf16[4,64,128]{2,1,0:T(8,128)(2,1)S(1)}, u32[]{:S(2)}) copy-start(bf16[4,64,128]{2,1,0:T(8,128)(2,1)S(1)} %convolution_convert_fusion.7) | copy-start | bytes 196612
  46.4 2.0 %copy-start.17 = (bf16[4,64,128]{2,1,0:T(8,128)(2,1)}, bf16[4,64,128]{2,1,0:T(8,128)(2,1)S(1)}, u32[]{:S(2)}) copy-start(bf16[4,64,128]{2,1,0:T(8,128)(2,1)S(1)} %convolution_convert_fusion.10) | copy-start | bytes 196612
  48.4 99.7 %reduce-scatter.13.cloned.1.call-start = ((), (), s32[]{:S(2)}) async-start(), calls=%async_computation.8 | async-start | bytes 2228224
  51.1 31.3 %copy-start.36 = (bf16[128,256]{0,1:T(8,128)(2,1)}, bf16[128,256]{0,1:T(8,128)(2,1)S(1)}, u32[]{:S(2)}) copy-start(bf16[128,256]{0,1:T(8,128)(2,1)S(1)} %copy.84) | copy-start | bytes 196612
  56.7 1.7 copy-start.23
  82.1 77.9 %reduce-scatter.9.cloned.1.call-start = ((), (), s32[]{:S(2)}) async-start(), calls=%async_computation.6 | async-start | bytes 196608 | tf_op jit(solution)/shard_map/reduce_scatter | solution.py:113
  84.4 5.7 %copy-start.8 = (f32[4,128,320]{1,2,0:T(8,128)S(1)}, f32[4,128,320]{1,2,0:T(8,128)}, u32[]{:S(2)}) copy-start(f32[4,128,320]{1,2,0:T(8,128)} %get-tuple-element.43) | copy-start | bytes 1966084
  84.4 5.7 %copy-start.30 = (bf16[320,256]{0,1:T(8,128)(2,1)S(1)}, bf16[320,256]{0,1:T(8,128)(2,1)}, u32[]{:S(2)}) copy-start(bf16[320,256]{0,1:T(8,128)(2,1)} %copy-done.29) | copy-start | bytes 491524
  84.4 5.7 %copy-start.37 = (bf16[128,256]{0,1:T(8,128)(2,1)S(1)}, bf16[128,256]{0,1:T(8,128)(2,1)}, u32[]{:S(2)}) copy-start(bf16[128,256]{0,1:T(8,128)(2,1)} %copy-done.36) | copy-start | bytes 196612
  85.7 23.3 %copy-start.2 = (f32[320,1024]{1,0:T(8,128)}, f32[320,1024]{1,0:T(8,128)S(1)}, u32[]{:S(2)}) copy-start(f32[320,1024]{1,0:T(8,128)S(1)} %pad_maximum_fusion.1) | copy-start | bytes 3932164
  86.5 8.2 %collective-permute-start.12 = (bf16[64,1024]{1,0:T(8,128)(2,1)}, bf16[64,1024]{1,0:T(8,128)(2,1)}, u32[]{:S(2)}, u32[]{:S(2)}) collective-permute-start(bf16[64,1024]{1,0:T(8,128)(2,1)} %slice.154), channel_id=1, source_target_pairs={{0,30},{2,0},{4,2},{6,4},{8,6},{10,8},{12,10},{14,12},{16,14},{18,... | collective-permute-start | bytes 393224 | tf_op jit(solution)/shard_map/ppermute | solution.py:16
  93.9 19.0 %copy-start.3 = (f32[320,1024]{1,0:T(8,128)}, f32[320,1024]{1,0:T(8,128)S(1)}, u32[]{:S(2)}) copy-start(f32[320,1024]{1,0:T(8,128)S(1)} %pad_maximum_fusion) | copy-start | bytes 3932164
  93.9 4.6 %collective-permute-start.8 = (bf16[64,1024]{1,0:T(8,128)(2,1)S(1)}, bf16[64,1024]{1,0:T(8,128)(2,1)S(1)}, u32[]{:S(2)}, u32[]{:S(2)}) collective-permute-start(bf16[64,1024]{1,0:T(8,128)(2,1)S(1)} %slice.155), channel_id=1, source_target_pairs={{0,30},{2,0},{4,2},{6,4},{8,6},{10,8},{12,10},{14,12},{16,14},{18,... | collective-permute-start | bytes 393224 | tf_op jit(solution)/shard_map/ppermute | solution.py:16
  95.6 6.3 %collective-permute-start.13 = (bf16[64,1024]{1,0:T(8,128)(2,1)S(1)}, bf16[64,1024]{1,0:T(8,128)(2,1)S(1)}, u32[]{:S(2)}, u32[]{:S(2)}) collective-permute-start(bf16[64,1024]{1,0:T(8,128)(2,1)S(1)} %fusion.19), channel_id=1, source_target_pairs={{0,30},{2,0},{4,2},{6,4},{8,6},{10,8},{12,10},{14,12},{16,14},{18,... | collective-permute-start | bytes 393224 | tf_op jit(solution)/shard_map/ppermute | solution.py:16
  98.6 19.8 %copy-start.26 = (bf16[128,256]{1,0:T(8,128)(2,1)S(1)}, bf16[128,256]{1,0:T(8,128)(2,1)}, u32[]{:S(2)}) copy-start(bf16[128,256]{1,0:T(8,128)(2,1)} %copy.89) | copy-start | bytes 196612
  98.6 19.8 %copy-start.27 = (bf16[128,256]{1,0:T(8,128)(2,1)S(1)}, bf16[128,256]{1,0:T(8,128)(2,1)}, u32[]{:S(2)}) copy-start(bf16[128,256]{1,0:T(8,128)(2,1)} %copy.90) | copy-start | bytes 196612
  98.6 19.8 %copy-start.28 = (bf16[128,256]{1,0:T(8,128)(2,1)S(1)}, bf16[128,256]{1,0:T(8,128)(2,1)}, u32[]{:S(2)}) copy-start(bf16[128,256]{1,0:T(8,128)(2,1)} %copy.91) | copy-start | bytes 196612
  98.6 7.1 %collective-permute-start.9 = (bf16[64,1024]{1,0:T(8,128)(2,1)S(1)}, bf16[64,1024]{1,0:T(8,128)(2,1)S(1)}, u32[]{:S(2)}, u32[]{:S(2)}) collective-permute-start(bf16[64,1024]{1,0:T(8,128)(2,1)S(1)} %fusion.23), channel_id=1, source_target_pairs={{0,30},{2,0},{4,2},{6,4},{8,6},{10,8},{12,10},{14,12},{16,14},{18,... | collective-permute-start | bytes 393224 | tf_op jit(solution)/shard_map/ppermute | solution.py:16
  101.9 7.1 %collective-permute-start.14 = (bf16[64,1024]{1,0:T(8,128)(2,1)S(1)}, bf16[64,1024]{1,0:T(8,128)(2,1)S(1)}, u32[]{:S(2)}, u32[]{:S(2)}) collective-permute-start(bf16[64,1024]{1,0:T(8,128)(2,1)S(1)} %fusion.18), channel_id=1, source_target_pairs={{0,30},{2,0},{4,2},{6,4},{8,6},{10,8},{12,10},{14,12},{16,14},{18,... | collective-permute-start | bytes 393224 | tf_op jit(solution)/shard_map/ppermute | solution.py:16
  105.7 7.2 %collective-permute-start.10 = (bf16[64,1024]{1,0:T(8,128)(2,1)S(1)}, bf16[64,1024]{1,0:T(8,128)(2,1)S(1)}, u32[]{:S(2)}, u32[]{:S(2)}) collective-permute-start(bf16[64,1024]{1,0:T(8,128)(2,1)S(1)} %fusion.22), channel_id=1, source_target_pairs={{0,30},{2,0},{4,2},{6,4},{8,6},{10,8},{12,10},{14,12},{16,14},{18,... | collective-permute-start | bytes 393224 | tf_op jit(solution)/shard_map/ppermute | solution.py:16
  109.1 12.8 %copy-start.1 = (bf16[1024,1024]{1,0:T(8,128)(2,1)S(1)}, bf16[1024,1024]{1,0:T(8,128)(2,1)}, u32[]{:S(2)}) copy-start(bf16[1024,1024]{1,0:T(8,128)(2,1)} %all-gather.2.cloned.1.call-done) | copy-start | bytes 6291460
  109.1 12.8 %copy-start.14 = (bf16[4,64,128]{2,1,0:T(8,128)(2,1)S(1)}, bf16[4,64,128]{2,1,0:T(8,128)(2,1)}, u32[]{:S(2)}) copy-start(bf16[4,64,128]{2,1,0:T(8,128)(2,1)} %copy-done.13) | copy-start | bytes 196612
  109.1 12.8 %copy-start.16 = (bf16[4,64,128]{2,1,0:T(8,128)(2,1)S(1)}, bf16[4,64,128]{2,1,0:T(8,128)(2,1)}, u32[]{:S(2)}) copy-start(bf16[4,64,128]{2,1,0:T(8,128)(2,1)} %copy-done.15) | copy-start | bytes 196612
  109.1 12.8 %copy-start.18 = (bf16[4,64,128]{2,1,0:T(8,128)(2,1)S(1)}, bf16[4,64,128]{2,1,0:T(8,128)(2,1)}, u32[]{:S(2)}) copy-start(bf16[4,64,128]{2,1,0:T(8,128)(2,1)} %copy-done.17) | copy-start | bytes 196612
  109.1 7.6 %collective-permute-start.15 = (bf16[64,1024]{1,0:T(8,128)(2,1)S(1)}, bf16[64,1024]{1,0:T(8,128)(2,1)S(1)}, u32[]{:S(2)}, u32[]{:S(2)}) collective-permute-start(bf16[64,1024]{1,0:T(8,128)(2,1)S(1)} %fusion.17), channel_id=1, source_target_pairs={{0,30},{2,0},{4,2},{6,4},{8,6},{10,8},{12,10},{14,12},{16,14},{18,... | collective-permute-start | bytes 393224 | tf_op jit(solution)/shard_map/ppermute | solution.py:16
  113.0 7.3 %collective-permute-start.11 = (bf16[64,1024]{1,0:T(8,128)(2,1)S(1)}, bf16[64,1024]{1,0:T(8,128)(2,1)S(1)}, u32[]{:S(2)}, u32[]{:S(2)}) collective-permute-start(bf16[64,1024]{1,0:T(8,128)(2,1)S(1)} %fusion.21), channel_id=1, source_target_pairs={{0,30},{2,0},{4,2},{6,4},{8,6},{10,8},{12,10},{14,12},{16,14},{18,... | collective-permute-start | bytes 393224 | tf_op jit(solution)/shard_map/ppermute | solution.py:16
  118.3 54.6 %reduce-scatter.7.cloned.1.call-start = ((), (), s32[]{:S(2)}) async-start(), calls=%async_computation.5 | async-start | bytes 196608 | tf_op jit(solution)/shard_map/reduce_scatter | solution.py:110
  (11 other events, 11.8 us)
Sparse Core Ops, SparseCore 0:
  9.6 35.8 all-gather.1
  48.5 30.9 reduce-scatter.10
  83.7 64.3 reduce-scatter.12
  150.8 9.2 reduce-scatter.8
  162.7 10.2 reduce-scatter.6
where the time goes:
time: 180 us; the launch traced here: 179 us
  waiting for transfers between devices  92.1 us (51%)
  starting transfers between devices  28.7 us (16%)
  matrix products  18.4 us (10%)
  local copies, waits for them, and re-layouts  17.7 us (10%)
  between operations  14.6 us (8%)
  other arithmetic  8.01 us (4%)
    ppermute x16, starting transfers between devices, shifted(): return lax.ppermute(value, axis, pairs)  28.3 us
    ppermute x16, waiting for transfers between devices, shifted(): return lax.ppermute(value, axis, pairs)  26.6 us
    unnamed x6, waiting for transfers between devices  25.8 us
    reduce_scatter x1, waiting for transfers between devices, local(): lax.psum_scatter(jnp.einsum('rc,re->ce', attended, out_grad, preferred_el...  16.6 us
    reduce_scatter x1, waiting for transfers between devices, local(): lax.psum_scatter(key_total.astype(jnp.bfloat16), 'tgt', scatter_dimension...  12.9 us
    reduce_scatter x1, waiting for transfers between devices, local(): lax.psum_scatter(value_total.astype(jnp.bfloat16), 'tgt', scatter_dimensi...  10.2 us
    unnamed x87, local copies, waits for them, and re-layouts  7.96 us
    sub x4, matrix products, head_block(): expo = jnp.exp(scores - top)  4.23 us
  transfers between devices with their start and end apart: 21, of which 13 were waited for; matrix products, arithmetic and copies ran while one was open for 21% of the time, Pallas kernels for 0%

commit v1 on v0

v1 whole, which is shorter than its diff:
```python
import functools

import jax
import jax.numpy as jnp
from jax import lax
from jax.experimental import pallas as pl
from jax.experimental.pallas import tpu as pltpu
from jax.sharding import PartitionSpec as P

HD = 64
WIN = 5
LANES = 128
BF = jnp.bfloat16
F32 = jnp.float32
MESH = pl.DeviceIdType.MESH


def dot(a, b, ca, cb):
    return lax.dot_general(a, b, (((ca,), (cb,)), ((), ())), preferred_element_type=F32)


def kernel(
    N,
    T,
    nbits,
    q_ref,
    k_ref,
    v_ref,
    w_ref,
    og_ref,
    out_ref,
    qg_ref,
    kg_ref,
    vg_ref,
    wgt_ref,
    qall,
    ogall,
    ogt,
    kall,
    vall,
    ag,
    att,
    qgs,
    kvown,
    kvs,
    kvr,
    outs,
    outr,
    outown,
    *rest,
):
    acc = rest[:nbits]
    ws = rest[nbits : 2 * nbits]
    wr = rest[2 * nbits : 3 * nbits]
    q_ss, q_rs, og_ss, og_rs, kv_ss, kv_rs, kvg_ss, kvg_rs, qg_ss, qg_rs, o_ss, o_rs, w_ss, w_rs = rest[
        3 * nbits :
    ]
    b = lax.axis_index("blk")
    t = lax.axis_index("tgt")
    rows, D = q_ref.shape
    Dt = w_ref.shape[0]
    R = rows * T
    src = k_ref.shape[0]
    pairs = Dt // LANES
    EB = D // N
    scale = HD ** (-0.5)

    def blk_at(step):
        return lax.rem(b + step + N, N)

    def tgt_at(step):
        return lax.rem(t + step + T, T)

    def bit(k):
        return lax.rem(b // (1 << k), 2)

    def mirror(k):
        return b + (1 - 2 * bit(k)) * (1 << k)

    def cols(tt):
        return pl.ds(pl.multiple_of(tt * Dt, LANES), Dt)

    def tile(tt):
        return pl.ds(pl.multiple_of(tt * rows, LANES), rows)

    def lanes(p, base=0):
        return pl.ds(pl.multiple_of(base + p * LANES, LANES), LANES)

    def remote(src_, dst_, ss, rs, dev):
        return pltpu.make_async_remote_copy(
            src_ref=src_, dst_ref=dst_, send_sem=ss, recv_sem=rs, device_id=dev, device_id_type=MESH
        )

    def q_copy(d):
        other = tgt_at(d)
        return remote(q_ref.at[:, cols(other)], qall.at[tile(t), :], q_ss.at[d], q_rs.at[d], (b, other))

    def og_copy(d):
        return remote(og_ref, ogall.at[tile(t), :], og_ss.at[d], og_rs.at[d], (b, tgt_at(d)))

    def kv_copy(i, w):
        ref, dst = ((k_ref, kall), (v_ref, vall))[i]
        return remote(
            ref.at[:, cols(t)],
            dst.at[pl.ds(w * src, src), :],
            kv_ss.at[i, w],
            kv_rs.at[i, w],
            (blk_at(w), t),
        )

    def kvg_copy(p, w):
        return remote(
            kvs.at[w - 1, :, :, lanes(p)],
            kvr.at[w - 1, :, :, lanes(p)],
            kvg_ss.at[p, w],
            kvg_rs.at[p, w],
            (blk_at(-w), t),
        )

    def qg_copy(p, d):
        other = tgt_at(d)
        return remote(
            qgs.at[tile(other), lanes(p)],
            qg_ref.at[:, lanes(p, t * Dt)],
            qg_ss.at[p, d],
            qg_rs.at[p, d],
            (b, other),
        )

    def o_copy(d):
        return remote(outs.at[d - 1], outr.at[d - 1], o_ss.at[d], o_rs.at[d], (b, tgt_at(d)))

    def w_copy(k, p):
        return remote(ws[k].at[p], wr[k].at[p], w_ss.at[k, p], w_rs.at[k, p], (mirror(k), t))

    barrier = pltpu.get_barrier_semaphore()
    peers = [(b, tgt_at(d)) for d in range(1, T)]
    for w in range(1, WIN):
        peers += [(blk_at(w), t), (blk_at(-w), t)]
    for k in range(3, nbits):
        peers.append((mirror(k), t))
    for peer in peers:
        pl.semaphore_signal(barrier, inc=1, device_id=peer, device_id_type=MESH)
    pl.semaphore_wait(barrier, len(peers))

    for d in range(1, T):
        og_copy(d).start()
    for w in range(WIN - 1, 0, -1):
        kv_copy(0, w).start()
        kv_copy(1, w).start()
    for d in range(1, T):
        q_copy(d).start()

    def project(tt):
        part = ogall[tile(tt), :]
        ag[tile(tt), :] = dot(part, w_ref[...], 1, 1).astype(BF)
        ogt[:, tile(tt)] = part.astype(F32).T.astype(BF)

    ogall[tile(t), :] = og_ref[...]
    qall[tile(t), :] = q_ref[:, cols(t)]
    kall[pl.ds(0, src), :] = k_ref[:, cols(t)]
    vall[pl.ds(0, src), :] = v_ref[:, cols(t)]
    project(t)
    for d in range(1, T):
        og_copy(d).wait_recv()
        project(tgt_at(-d))
    for d in range(1, T):
        q_copy(d).wait_recv()
    for w in range(WIN - 1, 0, -1):
        kv_copy(0, w).wait_recv()
        kv_copy(1, w).wait_recv()

    half = lax.broadcasted_iota(jnp.int32, (1, LANES), 1) // HD

    def fold(k, p):
        w_copy(k, p).wait_recv()
        value = acc[k][p, :, bit(k)] + wr[k][p].astype(F32)
        if k + 1 < nbits:
            acc[k + 1][p] = value.reshape(N >> (k + 2), 2, EB, LANES)
            ws[k + 1][p] = acc[k + 1][p, :, 1 - bit(k + 1)].astype(BF)
            w_copy(k + 1, p).start()
        else:
            wgt_ref[:, lanes(p)] = value[0].astype(BF)

    def pair(p, carry):
        c = lanes(p)
        kp, vp, qp, gp = kall[:, c], vall[:, c], qall[:, c], ag[:, c]
        att_t = jnp.zeros((LANES, R), F32)
        qg_t = jnp.zeros((LANES, R), F32)
        kg = jnp.zeros((WIN * src, LANES), F32)
        vg = jnp.zeros((WIN * src, LANES), F32)
        for i in range(2):
            mask = (half == i).astype(F32).astype(BF)
            km, vm, qm, gm = kp * mask, vp * mask, qp * mask, gp * mask
            scores = dot(km, qp, 1, 1) * scale
            expo = jnp.exp(scores - jnp.max(scores, axis=0, keepdims=True))
            probs = expo * (1.0 / jnp.sum(expo, axis=0, keepdims=True))
            low = probs.astype(BF)
            prob_grad = dot(vm, gp, 1, 1)
            center = jnp.sum(probs * prob_grad, axis=0, keepdims=True)
            score_grad = (scale * probs * (prob_grad - center)).astype(BF)
            att_t += dot(vm, low, 0, 0)
            qg_t += dot(km, score_grad, 0, 0)
            kg += dot(score_grad, qm, 1, 0)
            vg += dot(low, gm, 1, 0)
        att_low = att_t.astype(BF)
        grad = dot(ogt[...], att_low, 1, 1)
        acc[0][p] = grad.reshape(N // 2, 2, EB, LANES)
        ws[0][p] = acc[0][p, :, 1 - bit(0)].astype(BF)
        w_copy(0, p).start()
        kvown[0, :, c] = kg[:src]
        kvown[1, :, c] = vg[:src]
        for w in range(1, WIN):
            kvs[w - 1, 0, :, c] = kg[w * src : (w + 1) * src].astype(BF)
            kvs[w - 1, 1, :, c] = vg[w * src : (w + 1) * src].astype(BF)
            kvg_copy(p, w).start()
        qgs[:, c] = qg_t.T.astype(BF)
        for d in range(1, T):
            qg_copy(p, d).start()
        att[:, c] = att_t.T.astype(BF)

        @pl.when(p >= 1)
        def _():
            fold(0, p - 1)

        @pl.when(p >= 2)
        def _():
            fold(1, p - 2)

        return carry

    lax.fori_loop(0, pairs, pair, 0)

    fold(0, pairs - 1)
    for d in range(1, T):
        outs[d - 1] = dot(att[tile(tgt_at(d)), :], w_ref[...], 1, 0).astype(BF)
        o_copy(d).start()
    for p in range(max(pairs - 2, 0), pairs):
        fold(1, p)
    outown[...] = dot(att[tile(t), :], w_ref[...], 1, 0)
    qg_ref[:, cols(t)] = qgs[tile(t), :]
    for k in range(2, nbits):
        for p in range(pairs):
            fold(k, p)
        if k == 2:
            for p in range(pairs):
                for w in range(1, WIN):
                    kvg_copy(p, w).wait_recv()
            for i, ref in enumerate((kg_ref, vg_ref)):
                total = kvown[i]
                for w in range(1, WIN):
                    total += kvr[w - 1, i].astype(F32)
                ref[...] = total.astype(BF)
    total = outown[...]
    for d in range(1, T):
        o_copy(d).wait_recv()
        total += outr[d - 1].astype(F32)
    out_ref[...] = total.astype(BF)
    for p in range(pairs):
        for d in range(1, T):
            qg_copy(p, d).wait_recv()

    for d in range(1, T):
        og_copy(d).wait_send()
        q_copy(d).wait_send()
        o_copy(d).wait_send()
    for w in range(1, WIN):
        kv_copy(0, w).wait_send()
        kv_copy(1, w).wait_send()
    for p in range(pairs):
        for w in range(1, WIN):
            kvg_copy(p, w).wait_send()
        for d in range(1, T):
            qg_copy(p, d).wait_send()
        for k in range(nbits):
            w_copy(k, p).wait_send()


def local(queries, keys, values, out_weight, out_grad):
    N = lax.axis_size("blk")
    T = lax.axis_size("tgt")
    nbits = N.bit_length() - 1
    rows, D = queries.shape
    src = keys.shape[0]
    Dt = out_weight.shape[0]
    R = rows * T
    pairs = Dt // LANES
    EB = D // N
    halves = [(pairs, N >> (k + 1), EB, LANES) for k in range(nbits)]
    scratch = [
        pltpu.VMEM((R, Dt), BF),
        pltpu.VMEM((R, D), BF),
        pltpu.VMEM((D, R), BF),
        pltpu.VMEM((WIN * src, Dt), BF),
        pltpu.VMEM((WIN * src, Dt), BF),
        pltpu.VMEM((R, Dt), BF),
        pltpu.VMEM((R, Dt), BF),
        pltpu.VMEM((R, Dt), BF),
        pltpu.VMEM((2, src, Dt), F32),
        pltpu.VMEM((WIN - 1, 2, src, Dt), BF),
        pltpu.VMEM((WIN - 1, 2, src, Dt), BF),
        pltpu.VMEM((T - 1, rows, D), BF),
        pltpu.VMEM((T - 1, rows, D), BF),
        pltpu.VMEM((rows, D), F32),
    ]
    scratch += [pltpu.VMEM((h[0], h[1], 2, EB, LANES), F32) for h in halves]
    scratch += [pltpu.VMEM(h, BF) for h in halves]
    scratch += [pltpu.VMEM(h, BF) for h in halves]
    for shape in ((T,), (T,), (2, WIN), (pairs, WIN), (pairs, T), (T,), (nbits, pairs)):
        scratch += [pltpu.SemaphoreType.DMA(shape)] * 2
    vmem = pl.BlockSpec(memory_space=pltpu.VMEM)
    out, qg, kg, vg, wgt = pl.pallas_call(
        functools.partial(kernel, N, T, nbits),
        out_shape=(
            jax.ShapeDtypeStruct((rows, D), BF),
            jax.ShapeDtypeStruct((rows, D), BF),
            jax.ShapeDtypeStruct((src, Dt), BF),
            jax.ShapeDtypeStruct((src, Dt), BF),
            jax.ShapeDtypeStruct((EB, Dt), BF),
        ),
        in_specs=[vmem] * 5,
        out_specs=(vmem,) * 5,
        scratch_shapes=scratch,
        compiler_params=pltpu.CompilerParams(
            collective_id=0, has_side_effects=True, vmem_limit_bytes=48 * 1024 * 1024
        ),
    )(queries, keys, values, out_weight, out_grad)
    return out, qg, kg, vg, wgt.T


def solution(mesh):
    return jax.shard_map(
        local,
        mesh=mesh,
        in_specs=(
            P(("blk", "tgt"), None),
            P("blk", None),
            P("blk", None),
            P("tgt", None),
            P(("blk", "tgt"), None),
        ),
        out_specs=(
            P(("blk", "tgt"), None),
            P(("blk", "tgt"), None),
            P("blk", "tgt"),
            P("blk", "tgt"),
            P("tgt", "blk"),
        ),
        check_vma=False,
    )
```

time: 180 us -> 48.3 us (0.27)
  waiting for transfers between devices: 92.1 us -> 0 us
  Pallas kernels: 0 us -> 39.2 us
  starting transfers between devices: 28.7 us -> 0 us
  matrix products: 18.4 us -> 0 us
  between operations: 14.6 us -> 0.66 us
  local copies, waits for them, and re-layouts: 17.7 us -> 8.22 us
  other arithmetic: 8.01 us -> 0 us
    reduce_scatter x3 -> x0, waiting for transfers between devices: 39.7 us -> none  [the longest x1 16.6 us: local(): lax.psum_scatter(jnp.einsum('rc,re->ce', attended, out_grad, preferred_el...]
    pallas_call x0 -> x1, Pallas kernels: none -> 39.2 us  [local(): pl.pallas_call(functools.partial(kernel, N, T, nbits), out_shape=(jax.Sha...]
    ppermute x16 -> x0, starting transfers between devices: 28.3 us -> none  [shifted(): return lax.ppermute(value, axis, pairs)]
    ppermute x16 -> x0, waiting for transfers between devices: 26.6 us -> none  [shifted(): return lax.ppermute(value, axis, pairs)]
    unnamed x6 -> x0, waiting for transfers between devices: 25.8 us -> none
    dot_general x23 -> x0, matrix products: 14.2 us -> none  [the longest x1 2.42 us: local(): jnp.dot(out_grad, full_weight.T, preferred_element_type=jnp.float32)]
    convert_element_type x12 -> x0, other arithmetic: 4.83 us -> none  [the longest x1 1.63 us: local(): value_total.astype(jnp.bfloat16)]
    sub x4 -> x0, matrix products: 4.23 us -> none  [head_block(): expo = jnp.exp(scores - top)]
  transfers between devices with their start and end apart: 21 -> 0, of which waited for: 13 -> 0; matrix products, arithmetic and copies ran while one was open for 21% -> 0% of each run, Pallas kernels for 0% -> 0%
where the time goes in v1:
time: 48.3 us; the launch traced here: 48.1 us
  Pallas kernels  39.2 us (81%)
  local copies, waits for them, and re-layouts  8.22 us (17%)
  between operations  0.66 us (1%)
    pallas_call x1, Pallas kernels, local(): pl.pallas_call(functools.partial(kernel, N, T, nbits), out_shape=(jax.Sha...  39.2 us
    unnamed x15, local copies, waits for them, and re-layouts  8.22 us

profile of v1, /device:TPU:0, one launch (start us, length us, event | category | flops | bytes accessed | tf_op | source)
XLA Modules:
  0.0 48.1 jit_solution(4310512694088867991)
XLA Ops:
  0.6 0.0 copy-start
  0.6 1.2 %copy-done = bf16[512,1024]{1,0:T(8,128)(2,1)S(1)} copy-done((bf16[512,1024]{1,0:T(8,128)(2,1)S(1)}, bf16[512,1024]{1,0:T(8,128)(2,1)}, u32[]{:S(2)}) %copy-start) | copy-done | bytes 1048600
  1.9 0.0 copy-start.1
  1.9 0.9 %copy-done.1 = bf16[128,1024]{1,0:T(8,128)(2,1)S(1)} copy-done((bf16[128,1024]{1,0:T(8,128)(2,1)S(1)}, bf16[128,1024]{1,0:T(8,128)(2,1)}, u32[]{:S(2)}) %copy-start.1) | copy-done | bytes 262168
  2.8 0.0 copy-start.2
  2.8 0.9 %copy-done.2 = bf16[128,1024]{1,0:T(8,128)(2,1)S(1)} copy-done((bf16[128,1024]{1,0:T(8,128)(2,1)S(1)}, bf16[128,1024]{1,0:T(8,128)(2,1)}, u32[]{:S(2)}) %copy-start.2) | copy-done | bytes 262168
  3.8 0.0 copy-start.3
  3.8 0.9 %copy-done.3 = bf16[64,1024]{1,0:T(8,128)(2,1)S(1)} copy-done((bf16[64,1024]{1,0:T(8,128)(2,1)S(1)}, bf16[64,1024]{1,0:T(8,128)(2,1)}, u32[]{:S(2)}) %copy-start.3) | copy-done | bytes 131096
  4.7 0.0 copy-start.4
  4.7 0.9 %copy-done.4 = bf16[64,1024]{1,0:T(8,128)(2,1)S(1)} copy-done((bf16[64,1024]{1,0:T(8,128)(2,1)S(1)}, bf16[64,1024]{1,0:T(8,128)(2,1)}, u32[]{:S(2)}) %copy-start.4) | copy-done | bytes 131096
  5.6 39.2 %shard_map.92 = (bf16[128,1024]{1,0:T(8,128)(2,1)S(1)}, bf16[128,1024]{1,0:T(8,128)(2,1)S(1)}, bf16[64,512]{1,0:T(8,128)(2,1)S(1)}, bf16[64,512]{1,0:T(8,128)(2,1)S(1)}, bf16[64,512]{1,0:T(8,128)(2,1)S(1)}) custom-call(bf16[128,1024]{1,0:T(8,128)(2,1)S(1)} %copy-done.1, bf16[64,1024]{1,0:T(8,128)(2,1)S(1)} %copy-done.3, bf16[64,1024]{1,0:T(8,128)(2,1)S(1)} %copy-done.4, ...), custom_call_target="tpu_custom_call" | custom-call | tf_op jit(solution)/shard_map/pallas_call | solution.py:312
  44.8 0.7 %copy.15 = bf16[128,1024]{1,0:T(8,128)(2,1)} copy(bf16[128,1024]{1,0:T(8,128)(2,1)S(1)} %get-tuple-element.20) | data formatting | bytes 524288
  45.5 0.7 %copy.16 = bf16[128,1024]{1,0:T(8,128)(2,1)} copy(bf16[128,1024]{1,0:T(8,128)(2,1)S(1)} %get-tuple-element.21) | data formatting | bytes 524288
  46.2 0.6 %copy.17 = bf16[64,512]{1,0:T(8,128)(2,1)} copy(bf16[64,512]{1,0:T(8,128)(2,1)S(1)} %get-tuple-element.22) | data formatting | bytes 131072
  46.8 0.6 %copy.18 = bf16[64,512]{1,0:T(8,128)(2,1)} copy(bf16[64,512]{1,0:T(8,128)(2,1)S(1)} %get-tuple-element.23) | data formatting | bytes 131072
  47.4 0.6 %copy.19 = bf16[512,64]{0,1:T(8,128)(2,1)} copy(bf16[512,64]{0,1:T(8,128)(2,1)S(1)} %bitcast.1) | data formatting | bytes 131072
Async XLA Ops:
  0.6 1.2 %copy-start = (bf16[512,1024]{1,0:T(8,128)(2,1)S(1)}, bf16[512,1024]{1,0:T(8,128)(2,1)}, u32[]{:S(2)}) copy-start(bf16[512,1024]{1,0:T(8,128)(2,1)} %w_ref.1) | copy-start | bytes 3145732
  1.9 0.9 %copy-start.1 = (bf16[128,1024]{1,0:T(8,128)(2,1)S(1)}, bf16[128,1024]{1,0:T(8,128)(2,1)}, u32[]{:S(2)}) copy-start(bf16[128,1024]{1,0:T(8,128)(2,1)} %q_ref.1) | copy-start | bytes 786436
  2.8 0.9 %copy-start.2 = (bf16[128,1024]{1,0:T(8,128)(2,1)S(1)}, bf16[128,1024]{1,0:T(8,128)(2,1)}, u32[]{:S(2)}) copy-start(bf16[128,1024]{1,0:T(8,128)(2,1)} %og_ref.1) | copy-start | bytes 786436
  3.8 0.9 %copy-start.3 = (bf16[64,1024]{1,0:T(8,128)(2,1)S(1)}, bf16[64,1024]{1,0:T(8,128)(2,1)}, u32[]{:S(2)}) copy-start(bf16[64,1024]{1,0:T(8,128)(2,1)} %k_ref.1) | copy-start | bytes 393220
  4.7 0.9 %copy-start.4 = (bf16[64,1024]{1,0:T(8,128)(2,1)S(1)}, bf16[64,1024]{1,0:T(8,128)(2,1)}, u32[]{:S(2)}) copy-start(bf16[64,1024]{1,0:T(8,128)(2,1)} %v_ref.1) | copy-start | bytes 393220

commit v2 on v1

--- a/solution.py
+++ b/solution.py
@@ -38,6 +38,8 @@
     ogt,
     kall,
     vall,
+    wv,
+    in_s,
     ag,
     att,
     qgs,
@@ -133,6 +135,21 @@
     def w_copy(k, p):
         return remote(ws[k].at[p], wr[k].at[p], w_ss.at[k, p], w_rs.at[k, p], (mirror(k), t))
 
+    own = [
+        pltpu.make_async_copy(s, d, in_s.at[i])
+        for i, (s, d) in enumerate(
+            (
+                (og_ref, ogall.at[tile(t), :]),
+                (w_ref, wv),
+                (q_ref.at[:, cols(t)], qall.at[tile(t), :]),
+                (k_ref.at[:, cols(t)], kall.at[pl.ds(0, src), :]),
+                (v_ref.at[:, cols(t)], vall.at[pl.ds(0, src), :]),
+            )
+        )
+    ]
+    for copy in own:
+        copy.start()
+
     barrier = pltpu.get_barrier_semaphore()
     peers = [(b, tgt_at(d)) for d in range(1, T)]
     for w in range(1, WIN):
@@ -153,13 +170,11 @@
 
     def project(tt):
         part = ogall[tile(tt), :]
-        ag[tile(tt), :] = dot(part, w_ref[...], 1, 1).astype(BF)
+        ag[tile(tt), :] = dot(part, wv[...], 1, 1).astype(BF)
         ogt[:, tile(tt)] = part.astype(F32).T.astype(BF)
 
-    ogall[tile(t), :] = og_ref[...]
-    qall[tile(t), :] = q_ref[:, cols(t)]
-    kall[pl.ds(0, src), :] = k_ref[:, cols(t)]
-    vall[pl.ds(0, src), :] = v_ref[:, cols(t)]
+    for copy in own:
+        copy.wait()
     project(t)
     for d in range(1, T):
         og_copy(d).wait_recv()
@@ -233,11 +248,11 @@
 
     fold(0, pairs - 1)
     for d in range(1, T):
-        outs[d - 1] = dot(att[tile(tgt_at(d)), :], w_ref[...], 1, 0).astype(BF)
+        outs[d - 1] = dot(att[tile(tgt_at(d)), :], wv[...], 1, 0).astype(BF)
         o_copy(d).start()
     for p in range(max(pairs - 2, 0), pairs):
         fold(1, p)
-    outown[...] = dot(att[tile(t), :], w_ref[...], 1, 0)
+    outown[...] = dot(att[tile(t), :], wv[...], 1, 0)
     qg_ref[:, cols(t)] = qgs[tile(t), :]
     for k in range(2, nbits):
         for p in range(pairs):
@@ -274,6 +289,14 @@
             qg_copy(p, d).wait_send()
         for k in range(nbits):
             w_copy(k, p).wait_send()
+
+
+def store_kernel(*refs):
+    copies = [pltpu.make_async_copy(refs[i], refs[5 + i], refs[10].at[i]) for i in range(5)]
+    for copy in copies:
+        copy.start()
+    for copy in copies:
+        copy.wait()
 
 
 def local(queries, keys, values, out_weight, out_grad):
@@ -293,6 +316,8 @@
         pltpu.VMEM((D, R), BF),
         pltpu.VMEM((WIN * src, Dt), BF),
         pltpu.VMEM((WIN * src, Dt), BF),
+        pltpu.VMEM((Dt, D), BF),
+        pltpu.SemaphoreType.DMA((5,)),
         pltpu.VMEM((R, Dt), BF),
         pltpu.VMEM((R, Dt), BF),
         pltpu.VMEM((R, Dt), BF),
@@ -318,13 +343,21 @@
             jax.ShapeDtypeStruct((src, Dt), BF),
             jax.ShapeDtypeStruct((EB, Dt), BF),
         ),
-        in_specs=[vmem] * 5,
+        in_specs=[pl.BlockSpec(memory_space=pltpu.HBM)] * 5,
         out_specs=(vmem,) * 5,
         scratch_shapes=scratch,
         compiler_params=pltpu.CompilerParams(
-            collective_id=0, has_side_effects=True, vmem_limit_bytes=48 * 1024 * 1024
+            collective_id=0, has_side_effects=True, vmem_limit_bytes=64 * 1024 * 1024 - 64 * 1024
         ),
     )(queries, keys, values, out_weight, out_grad)
+    results = (out, qg, kg, vg, wgt)
+    out, qg, kg, vg, wgt = pl.pallas_call(
+        store_kernel,
+        out_shape=tuple(jax.ShapeDtypeStruct(r.shape, r.dtype) for r in results),
+        in_specs=[pl.BlockSpec(memory_space=pl.ANY)] * 5,
+        out_specs=(pl.BlockSpec(memory_space=pltpu.HBM),) * 5,
+        scratch_shapes=[pltpu.SemaphoreType.DMA((5,))],
+    )(*results)
     return out, qg, kg, vg, wgt.T
 
 

time: 48.3 us -> 64.2 us (1.33)
  Pallas kernels: 39.2 us -> 63.4 us
  local copies, waits for them, and re-layouts: 8.22 us -> 0 us
    pallas_call x0 -> x1, Pallas kernels: none -> 23 us  [local(): pl.pallas_call(store_kernel, out_shape=tuple((jax.ShapeDtypeStruct(r.shap...]
    unnamed x15 -> x0, local copies, waits for them, and re-layouts: 8.22 us -> none
    pallas_call x1, Pallas kernels: 39.2 us -> 40.4 us  [local(): pl.pallas_call(functools.partial(kernel, N, T, nbits), out_shape=(jax.Sha...]
where the time goes in v2:
time: 64.2 us; the launch traced here: 64 us
  Pallas kernels  63.4 us (99%)
    pallas_call x1, Pallas kernels, local(): pl.pallas_call(functools.partial(kernel, N, T, nbits), out_shape=(jax.Sha...  40.4 us
    pallas_call x1, Pallas kernels, local(): pl.pallas_call(store_kernel, out_shape=tuple((jax.ShapeDtypeStruct(r.shap...  23 us

profile of v2, /device:TPU:0, one launch (start us, length us, event | category | flops | bytes accessed | tf_op | source)
XLA Modules:
  0.0 64.0 jit_solution(12874398422567107972)
XLA Ops:
  0.6 40.4 %shard_map.92 = (bf16[128,1024]{1,0:T(8,128)(2,1)}, bf16[128,1024]{1,0:T(8,128)(2,1)}, bf16[64,512]{1,0:T(8,128)(2,1)}, bf16[64,512]{1,0:T(8,128)(2,1)}, bf16[64,512]{1,0:T(8,128)(2,1)}) custom-call(bf16[128,1024]{1,0:T(8,128)(2,1)} %q_ref.1, bf16[64,1024]{1,0:T(8,128)(2,1)} %k_ref.1, bf16[64,1024]{1,0:T(8,128)(2,1)} %v_ref.1, bf16[512,1024]{1,0:T(8,128)(2,1)} %w_ref.1, ...), custom_call_target="tpu_custom_call" | custom-call | tf_op jit(solution)/shard_map/pallas_call | solution.py:337
  41.0 23.0 %shard_map.93 = (bf16[128,1024]{1,0:T(8,128)(2,1)}, bf16[128,1024]{1,0:T(8,128)(2,1)}, bf16[64,512]{1,0:T(8,128)(2,1)}, bf16[64,512]{1,0:T(8,128)(2,1)}, bf16[64,512]{1,0:T(8,128)(2,1)}) custom-call(bf16[128,1024]{1,0:T(8,128)(2,1)} %get-tuple-element.15.refs_0_, bf16[128,1024]{1,0:T(8,128)(2,1)} %get-tuple-element.16.refs_1_, ...), custom_call_target="tpu_custom_call" | custom-call | tf_op jit(solution)/shard_map/pallas_call | solution.py:354

commit v3 on v2

--- a/solution.py
+++ b/solution.py
@@ -93,20 +93,26 @@
             src_ref=src_, dst_ref=dst_, send_sem=ss, recv_sem=rs, device_id=dev, device_id_type=MESH
         )
 
-    def q_copy(d):
+    def q_copy(p, d):
         other = tgt_at(d)
-        return remote(q_ref.at[:, cols(other)], qall.at[tile(t), :], q_ss.at[d], q_rs.at[d], (b, other))
+        return remote(
+            q_ref.at[:, lanes(p, other * Dt)],
+            qall.at[tile(t), lanes(p)],
+            q_ss.at[p, d],
+            q_rs.at[p, d],
+            (b, other),
+        )
 
     def og_copy(d):
         return remote(og_ref, ogall.at[tile(t), :], og_ss.at[d], og_rs.at[d], (b, tgt_at(d)))
 
-    def kv_copy(i, w):
+    def kv_copy(p, i, w):
         ref, dst = ((k_ref, kall), (v_ref, vall))[i]
         return remote(
-            ref.at[:, cols(t)],
-            dst.at[pl.ds(w * src, src), :],
-            kv_ss.at[i, w],
-            kv_rs.at[i, w],
+            ref.at[:, lanes(p, t * Dt)],
+            dst.at[pl.ds(w * src, src), lanes(p)],
+            kv_ss.at[p, i, w],
+            kv_rs.at[p, i, w],
             (blk_at(w), t),
         )
 
@@ -162,11 +168,12 @@
 
     for d in range(1, T):
         og_copy(d).start()
-    for w in range(WIN - 1, 0, -1):
-        kv_copy(0, w).start()
-        kv_copy(1, w).start()
-    for d in range(1, T):
-        q_copy(d).start()
+    for p in range(pairs):
+        for w in range(WIN - 1, 0, -1):
+            kv_copy(p, 0, w).start()
+            kv_copy(p, 1, w).start()
+        for d in range(1, T):
+            q_copy(p, d).start()
 
     def project(tt):
         part = ogall[tile(tt), :]
@@ -179,12 +186,6 @@
     for d in range(1, T):
         og_copy(d).wait_recv()
         project(tgt_at(-d))
-    for d in range(1, T):
-        q_copy(d).wait_recv()
-    for w in range(WIN - 1, 0, -1):
-        kv_copy(0, w).wait_recv()
-        kv_copy(1, w).wait_recv()
-
     half = lax.broadcasted_iota(jnp.int32, (1, LANES), 1) // HD
 
     def fold(k, p):
@@ -199,6 +200,11 @@
 
     def pair(p, carry):
         c = lanes(p)
+        for d in range(1, T):
+            q_copy(p, d).wait_recv()
+        for w in range(WIN - 1, 0, -1):
+            kv_copy(p, 0, w).wait_recv()
+            kv_copy(p, 1, w).wait_recv()
         kp, vp, qp, gp = kall[:, c], vall[:, c], qall[:, c], ag[:, c]
         att_t = jnp.zeros((LANES, R), F32)
         qg_t = jnp.zeros((LANES, R), F32)
@@ -277,26 +283,22 @@
 
     for d in range(1, T):
         og_copy(d).wait_send()
-        q_copy(d).wait_send()
         o_copy(d).wait_send()
-    for w in range(1, WIN):
-        kv_copy(0, w).wait_send()
-        kv_copy(1, w).wait_send()
     for p in range(pairs):
         for w in range(1, WIN):
+            kv_copy(p, 0, w).wait_send()
+            kv_copy(p, 1, w).wait_send()
             kvg_copy(p, w).wait_send()
         for d in range(1, T):
+            q_copy(p, d).wait_send()
             qg_copy(p, d).wait_send()
         for k in range(nbits):
             w_copy(k, p).wait_send()
 
 
 def store_kernel(*refs):
-    copies = [pltpu.make_async_copy(refs[i], refs[5 + i], refs[10].at[i]) for i in range(5)]
-    for copy in copies:
-        copy.start()
-    for copy in copies:
-        copy.wait()
+    for i in range(5):
+        refs[5 + i][...] = refs[i][...]
 
 
 def local(queries, keys, values, out_weight, out_grad):
@@ -331,7 +333,7 @@
     scratch += [pltpu.VMEM((h[0], h[1], 2, EB, LANES), F32) for h in halves]
     scratch += [pltpu.VMEM(h, BF) for h in halves]
     scratch += [pltpu.VMEM(h, BF) for h in halves]
-    for shape in ((T,), (T,), (2, WIN), (pairs, WIN), (pairs, T), (T,), (nbits, pairs)):
+    for shape in ((pairs, T), (T,), (pairs, 2, WIN), (pairs, WIN), (pairs, T), (T,), (nbits, pairs)):
         scratch += [pltpu.SemaphoreType.DMA(shape)] * 2
     vmem = pl.BlockSpec(memory_space=pltpu.VMEM)
     out, qg, kg, vg, wgt = pl.pallas_call(
@@ -354,9 +356,8 @@
     out, qg, kg, vg, wgt = pl.pallas_call(
         store_kernel,
         out_shape=tuple(jax.ShapeDtypeStruct(r.shape, r.dtype) for r in results),
-        in_specs=[pl.BlockSpec(memory_space=pl.ANY)] * 5,
-        out_specs=(pl.BlockSpec(memory_space=pltpu.HBM),) * 5,
-        scratch_shapes=[pltpu.SemaphoreType.DMA((5,))],
+        in_specs=[vmem] * 5,
+        out_specs=(vmem,) * 5,
     )(*results)
     return out, qg, kg, vg, wgt.T
 

time: 64.2 us -> 41.3 us (0.64)
  Pallas kernels: 63.4 us -> 40.5 us
    pallas_call x1, Pallas kernels: 23 us -> 1.93 us  [local(): pl.pallas_call(store_kernel, out_shape=tuple((jax.ShapeDtypeStruct(r.shap...]
    pallas_call x1, Pallas kernels: 40.4 us -> 38.5 us  [local(): pl.pallas_call(functools.partial(kernel, N, T, nbits), out_shape=(jax.Sha...]
where the time goes in v3:
time: 41.3 us; the launch traced here: 41.1 us
  Pallas kernels  40.5 us (98%)
  between operations  0.64 us (2%)
    pallas_call x1, Pallas kernels, local(): pl.pallas_call(functools.partial(kernel, N, T, nbits), out_shape=(jax.Sha...  38.5 us
    pallas_call x1, Pallas kernels, local(): pl.pallas_call(store_kernel, out_shape=tuple((jax.ShapeDtypeStruct(r.shap...  1.93 us

profile of v3, /device:TPU:0, one launch (start us, length us, event | category | flops | bytes accessed | tf_op | source)
XLA Modules:
  0.0 41.1 jit_solution(6744171359075063866)
XLA Ops:
  0.6 38.5 %shard_map.92 = (bf16[128,1024]{1,0:T(8,128)(2,1)}, bf16[128,1024]{1,0:T(8,128)(2,1)}, bf16[64,512]{1,0:T(8,128)(2,1)}, bf16[64,512]{1,0:T(8,128)(2,1)}, bf16[64,512]{1,0:T(8,128)(2,1)}) custom-call(bf16[128,1024]{1,0:T(8,128)(2,1)} %q_ref.1, bf16[64,1024]{1,0:T(8,128)(2,1)} %k_ref.1, bf16[64,1024]{1,0:T(8,128)(2,1)} %v_ref.1, bf16[512,1024]{1,0:T(8,128)(2,1)} %w_ref.1, ...), custom_call_target="tpu_custom_call" | custom-call | tf_op jit(solution)/shard_map/pallas_call | solution.py:339
  39.2 1.9 %shard_map.93 = (bf16[128,1024]{1,0:T(8,128)(2,1)}, bf16[128,1024]{1,0:T(8,128)(2,1)}, bf16[64,512]{1,0:T(8,128)(2,1)}, bf16[64,512]{1,0:T(8,128)(2,1)}, bf16[64,512]{1,0:T(8,128)(2,1)}) custom-call(bf16[128,1024]{1,0:T(8,128)(2,1)} %get-tuple-element.15.refs_0_, bf16[128,1024]{1,0:T(8,128)(2,1)} %get-tuple-element.16.refs_1_, ...), custom_call_target="tpu_custom_call" | custom-call | tf_op jit(solution)/shard_map/pallas_call | solution.py:356
